TPU v7x, 128 devices: a whole 4x4x4 slice. The times are simulated.
128 devices in a mesh: seq: 32 (over x, z_hi, y), dp: 4 (over z_lo, core).
Axes of the slice: x: 4, y: 4, z: 4 (z_hi: 2, z_lo: 2; z = z_hi * 2 + z_lo), core: 2. Of those that a mesh axis runs over, the one named last changes fastest.
Arguments:
- tokens: bfloat16 [4, 32, 384, 1152], P('dp', 'seq'), may hold values from -6 to 6
- cotangent: bfloat16 [4, 32, 384, 1152], P('dp', 'seq'), may hold values from -6 to 6
- mask: int32 [4, 32, 384], P('dp'), may hold values 0 or 1
- t_index: int32 [4], P('dp'), may hold values from 1 to 15
- mod_table: float32 [16, 6, 1152], replicated, may hold values from -3 to 3
- wqkv_s: bfloat16 [1152, 1728], replicated
- wo_s: bfloat16 [576, 1152], replicated, may hold values from -0.25 to 0.25
- wqkv_t: bfloat16 [1152, 1728], replicated
- wo_t: bfloat16 [576, 1152], replicated, may hold values from -0.25 to 0.25
Outputs:
- grad_tokens: float32 [4, 32, 384, 1152], P('dp', 'seq')
- grad_wqkv_s: float32 [1152, 1728], P('seq')
- grad_wo_s: float32 [576, 1152], P('seq')
- grad_wqkv_t: float32 [1152, 1728], P('seq')
- grad_wo_t: float32 [576, 1152], P('seq')
All inputs are finite; a program needn't handle non-finite values. No bound on the sum of `mask` on one device may be relied on, other than what follows from the above.
Results may differ from a plain program's by a relative error of at most 0.039.
The roundings to bfloat16 on the way count: a program that leaves them out, or rounds other values in their place, can miss the bound.
Values may be sent and summed in bfloat16 or wider, within the bound.
No kernel may reach another device: no remote copies, remote signals or barrier semaphores. Data moves between devices by JAX's collectives and lax.ppermute only.
A program may use at most 128 MiB of HBM per device.

v0:
```python
import math

import jax
import jax.numpy as jnp
from jax import lax
from jax.sharding import PartitionSpec as P

H = 8
E = 72


def modulate(marks, row_clean, row_noised, base):
    chosen = (marks == 1)[..., None]
    shift_offset = jnp.where(chosen, row_clean[base], row_noised[base])
    scale_factor = jnp.where(chosen, row_clean[base + 1], row_noised[base + 1])
    gate_factor = jnp.where(chosen, row_clean[base + 2], row_noised[base + 2])
    return (shift_offset, scale_factor, gate_factor)


def softmax_bf(scores):
    top = jnp.max(scores, axis=-1, keepdims=True)
    expo = jnp.exp(scores - top)
    probs = expo / jnp.sum(expo, axis=-1, keepdims=True)
    return lax.optimization_barrier(probs.astype(jnp.bfloat16)).astype(jnp.float32)


def core_spatial(query_key_value):
    count, length, _ = query_key_value.shape
    width = H * E
    query = query_key_value[..., :width].astype(jnp.float32).reshape(count, length, H, E)
    keys = query_key_value[..., width : 2 * width].astype(jnp.float32).reshape(count, length, H, E)
    values = query_key_value[..., 2 * width :].astype(jnp.float32).reshape(count, length, H, E)
    scores = jnp.einsum("nqhe,nkhe->nhqk", query, keys) * E ** (-0.5)
    probs = softmax_bf(scores)
    head_split = jnp.einsum("nhqk,nkhe->nqhe", probs, values)
    return head_split.reshape(count, length, width).astype(jnp.bfloat16)


def core_temporal(query_key_value):
    length, count, _ = query_key_value.shape
    width = H * E
    query = query_key_value[..., :width].astype(jnp.float32).reshape(length, count, H, E)
    keys = query_key_value[..., width : 2 * width].astype(jnp.float32).reshape(length, count, H, E)
    values = query_key_value[..., 2 * width :].astype(jnp.float32).reshape(length, count, H, E)
    scores = jnp.einsum("qnhe,knhe->nhqk", query, keys) * E ** (-0.5)
    probs = softmax_bf(scores)
    head_split = jnp.einsum("nhqk,knhe->qnhe", probs, values)
    return head_split.reshape(length, count, width).astype(jnp.bfloat16)


def branch_forward(inputs, marks, row_clean, row_noised, base, wqkv, wout, core):
    shift_offset, scale_factor, gate_factor = modulate(marks, row_clean, row_noised, base)
    xfull = inputs.astype(jnp.float32)
    centered_input = xfull - jnp.mean(xfull, axis=-1, keepdims=True)
    inverse_deviation = lax.rsqrt(
        jnp.mean(centered_input * centered_input, axis=-1, keepdims=True) + 1e-06
    )
    normalized_input = centered_input * inverse_deviation
    norm_output = (normalized_input * (1.0 + scale_factor) + shift_offset).astype(jnp.bfloat16)
    query_key_value = jnp.dot(norm_output, wqkv, preferred_element_type=jnp.float32).astype(
        jnp.bfloat16
    )
    head_split = core(query_key_value)
    attn = jnp.dot(head_split, wout, preferred_element_type=jnp.float32)
    output_rows = (xfull + gate_factor * attn).astype(jnp.bfloat16)
    return (
        output_rows,
        (
            normalized_input,
            inverse_deviation,
            norm_output,
            query_key_value,
            head_split,
            gate_factor,
            scale_factor,
        ),
    )


def branch_backward(saved_residuals, wqkv, wout, core, dout):
    (
        normalized_input,
        inverse_deviation,
        norm_output,
        query_key_value,
        head_split,
        gate_factor,
        scale_factor,
    ) = saved_residuals
    dres = dout.astype(jnp.float32)
    dattn = (dres * gate_factor).astype(jnp.bfloat16)
    width = head_split.shape[-1]
    g_wo = lax.dot_general(
        head_split.reshape(-1, width),
        dattn.reshape(-1, dattn.shape[-1]),
        (((0,), (0,)), ((), ())),
        preferred_element_type=jnp.float32,
    )
    last = dattn.ndim - 1
    dheads = lax.dot_general(
        dattn, wout, (((last,), (1,)), ((), ())), preferred_element_type=jnp.float32
    ).astype(jnp.bfloat16)
    _, pull = jax.vjp(core, query_key_value)
    dqkv = pull(dheads)[0]
    g_wqkv = lax.dot_general(
        norm_output.reshape(-1, norm_output.shape[-1]),
        dqkv.reshape(-1, dqkv.shape[-1]),
        (((0,), (0,)), ((), ())),
        preferred_element_type=jnp.float32,
    )
    dnormed = lax.dot_general(
        dqkv, wqkv, (((last,), (1,)), ((), ())), preferred_element_type=jnp.float32
    )
    normalized_gradient = dnormed * (1.0 + scale_factor)
    line_gradient = inverse_deviation * (
        normalized_gradient
        - jnp.mean(normalized_gradient, axis=-1, keepdims=True)
        - normalized_input
        * jnp.mean(normalized_gradient * normalized_input, axis=-1, keepdims=True)
    )
    return (dres + line_gradient, g_wqkv, g_wo)


def body(tokens, cotangent, mask, t_index, mod_table, wqkv_s, wo_s, wqkv_t, wo_t):
    seq_count = lax.axis_size("seq")
    seq_rank = lax.axis_index("seq")
    frame_count = tokens.shape[1]
    patches = tokens.shape[2]
    patch_count = patches // seq_count
    row_clean = mod_table[0]
    row_noised = lax.dynamic_index_in_dim(mod_table, t_index[0], 0, keepdims=False)
    frame_marks = lax.dynamic_slice_in_dim(mask[0], seq_rank * frame_count, frame_count, 0)
    patch_marks = lax.dynamic_slice_in_dim(mask[0], seq_rank * patch_count, patch_count, 1)
    local_frames = tokens[0]
    middle, saved_s = branch_forward(
        local_frames, frame_marks, row_clean, row_noised, 0, wqkv_s, wo_s, core_spatial
    )
    middle_patch, dpatch = (
        lax.all_to_all(middle, "seq", split_axis=1, concat_axis=0, tiled=True),
        lax.all_to_all(cotangent[0], "seq", split_axis=1, concat_axis=0, tiled=True),
    )
    _, saved_t = branch_forward(
        middle_patch, patch_marks, row_clean, row_noised, 3, wqkv_t, wo_t, core_temporal
    )
    dmiddle_patch, gq_t, go_t = branch_backward(saved_t, wqkv_t, wo_t, core_temporal, dpatch)
    dmiddle = lax.all_to_all(dmiddle_patch, "seq", split_axis=0, concat_axis=1, tiled=True)
    dlocal, gq_s, go_s = branch_backward(saved_s, wqkv_s, wo_s, core_spatial, dmiddle)
    shares = (
        lax.psum_scatter(gq_s, "seq", scatter_dimension=0, tiled=True),
        lax.psum_scatter(go_s, "seq", scatter_dimension=0, tiled=True),
        lax.psum_scatter(gq_t, "seq", scatter_dimension=0, tiled=True),
        lax.psum_scatter(go_t, "seq", scatter_dimension=0, tiled=True),
    )
    summed = lax.psum((shares[0], shares[1], shares[2], shares[3]), "dp")
    factor = 1.0 / math.sqrt(lax.axis_size("dp") * frame_count * seq_count * patches)
    return (
        dlocal[None],
        summed[0] * factor,
        summed[1] * factor,
        summed[2] * factor,
        summed[3] * factor,
    )


def solution(mesh):
    return jax.shard_map(
        body,
        mesh=mesh,
        in_specs=(
            P("dp", "seq", None, None),
            P("dp", "seq", None, None),
            P("dp", None, None),
            P("dp"),
            P(),
            P(),
            P(),
            P(),
            P(),
        ),
        out_specs=(
            P("dp", "seq", None, None),
            P("seq", None),
            P("seq", None),
            P("seq", None),
            P("seq", None),
        ),
        check_vma=False,
    )
```

profile of v0, /device:TPU:1, one launch (start us, length us, event | category | flops | bytes accessed | tf_op | source)
XLA Modules:
  0.0 694.1 jit_solution(1974424697025215110)
XLA Ops:
  11.7 1.8 slice_reduce_fusion.2
  14.1 4.7 fusion.26
  21.9 3.8 convert_reduce_fusion
  31.4 6.9 reduce.50
  38.3 3.0 reshape.894
  41.3 11.5 %all-to-all-start.1 = ((bf16[32,2,6912]{2,1,0:T(2,128)(2,1)}), bf16[32,2,6912]{2,1,0:T(2,128)(2,1)}, u32[]{:S(2)}, u32[]{:S(2)}) async-start(bf16[32,2,6912]{2,1,0:T(2,128)(2,1)} %reshape.894), calls=%async_computation.1 | async-start | bytes 1769472 | tf_op jit(solution)/shard_map/all_to_all | solution.py:139
  54.9 2.5 copy.174
  57.5 6.9 reduce.51
  64.4 3.0 reshape.896
  69.9 9.7 %all-to-all-start = ((bf16[32,2,6912]{2,1,0:T(2,128)(2,1)}), bf16[32,2,6912]{2,1,0:T(2,128)(2,1)}, u32[]{:S(2)}, u32[]{:S(2)}) async-start(bf16[32,2,6912]{2,1,0:T(2,128)(2,1)} %reshape.896), calls=%async_computation | async-start | bytes 1769472 | tf_op jit(solution)/shard_map/all_to_all | solution.py:140
  79.6 5.0 reshape.895
  84.6 1.9 convert_reduce_fusion.5
  88.5 9.2 %convert_reduce_fusion.4 = (f32[384,1152]{1,0:T(8,128)}, f32[384]{0:T(512)}) fusion(f32[384]{0:T(512)} %broadcast_multiply_fusion.8, bf16[384,1,1152]{2,1,0:T(2,128)(2,1)S(1)} %reshape.895), kind=kLoop, calls=%fused_computation.86 | loop fusion | flops 1769088 | bytes 2657280 | tf_op jit(solution)/shard_map/convert_element_type | solution.py:53
  97.7 5.0 reshape.897
  102.7 6.2 convert_reduce_fusion.2
  109.0 3.0 reshape.865
  112.0 4.1 fusion.75
  116.0 2.6 reshape.857
  124.1 2.7 reshape.867
  126.8 5.4 fusion.22
  133.6 2.7 reshape.860
  136.2 2.6 reshape.859
  138.8 3.1 reshape.858
  141.9 2.0 convolution_convert_fusion.4
  149.6 1.8 fusion.74
  151.4 1.7 fusion.73
  153.2 8.2 %convert_reduce_fusion.3 = bf16[384,1152]{1,0:T(8,128)(2,1)} fusion(pred[384]{0:T(512)(128)(4,1)S(1)} %copy-done.59, f32[1152]{0:T(1024)S(1)} %copy-done.40, f32[1152]{0:T(1024)S(1)} %copy-done.39, bf16[384,1,1152]{2,1,0:T(2,128)(2,1)S(1)} %reshape.897), kind=kLoop, calls=%fused_computation.79 | loop fusion | flops 1769472 | bytes 1779072 | tf_op jit(solution)/shard_map/convert_element_type | solution.py:91
  161.3 2.3 convert_element_type.372
  172.2 5.8 fusion.152
  179.2 2.5 copy.111
  181.7 9.6 %all-to-all-start.2 = ((f32[32,12,1152]{2,1,0:T(8,128)}), f32[32,12,1152]{2,1,0:T(8,128)}, u32[]{:S(2)}, u32[]{:S(2)}) async-start(f32[32,12,1152]{2,1,0:T(8,128)} %copy.111), calls=%async_computation.2 | async-start | bytes 4718592 | tf_op jit(solution)/shard_map/all_to_all | solution.py:146
  191.4 3.6 convolution_bitcast_fusion.1
  195.1 6.0 convolution_bitcast_fusion
  201.1 21.3 %all-to-all-done.2 = f32[32,12,1152]{2,1,0:T(8,128)} async-done(((f32[32,12,1152]{2,1,0:T(8,128)}), f32[32,12,1152]{2,1,0:T(8,128)}, u32[]{:S(2)}, u32[]{:S(2)}) %all-to-all-start.2) | async-done | bytes 1769504 | tf_op jit(solution)/shard_map/all_to_all | solution.py:146
  222.4 2.8 all_to_all.11
  225.2 2.6 convolution_convert_fusion.6
  227.9 3.6 fusion.81
  235.2 1.9 fusion.87
  237.1 2.0 fusion.84
  239.1 1.9 multiply_convert_fusion
  241.2 3.4 fusion.160
  246.0 7.0 %fusion.66 = f32[1152,1728]{1,0:T(8,128)} fusion(bf16[1,1,384,1152]{3,2,1,0:T(8,128)(2,1)S(1)} %copy-done.8, f32[1152]{0:T(1024)S(1)} %copy-done.52, f32[1152]{0:T(1024)S(1)} %copy-done.54, f32[1152]{0:T(1024)S(1)} %copy-done.48, f32[1152]{0:T(1024)S(1)} %copy-done.50, f32[384]{0:T(512)S(1)} %copy-done.46, f32[384]{0:T(512)S(1)} %broadcast_multiply_fusion.9, ...), kind=kOutput, calls=%fused_computation.104 | convolution fusion | flops 1536786432 | bytes 10196352 | tf_op jit(solution)/shard_map/dot_general | solution.py:105
  253.0 283.0 %fusion.153 = (f32[40,1728]{1,0:T(8,128)S(1)}, f32[40,1728]{1,0:T(8,128)}) fusion(f32[1152,1728]{1,0:T(8,128)} %fusion.66, f32[1152,1728]{1,0:T(8,128)} %convolution_bitcast_fusion), kind=kCustom, calls=%all-reduce-scatter.2 | all-reduce-scatter fusion | flops 4423681 | bytes 16478720
  537.4 2.6 collective-permute-start.1
  540.0 4.2 collective-permute-start.3
  544.3 5.8 fusion.151
  550.1 4.2 collective-permute-start
  554.3 6.3 collective-permute-start.6
  560.6 4.5 collective-permute-start.5
  565.1 6.9 %collective-permute-start.4 = (f32[40,1728]{1,0:T(8,128)}, f32[40,1728]{1,0:T(8,128)}, u32[]{:S(2)}, u32[]{:S(2)}) collective-permute-start(f32[40,1728]{1,0:T(8,128)} %get-tuple-element.32), channel_id=1, source_target_pairs={{0,4},{4,8},{8,12},{12,16},{16,20},{20,24},{24,28},{28,32},{32,36}... | collective-permute-start | bytes 829448
  572.9 4.3 collective-permute-start.7
  577.2 4.3 concatenate
  581.5 12.5 %collective-permute-done.7 = f32[4,1728]{1,0:T(4,128)S(1)} collective-permute-done((f32[4,1728]{1,0:T(4,128)S(1)}, f32[4,1728]{1,0:T(4,128)S(1)}, u32[]{:S(2)}, u32[]{:S(2)}) %collective-permute-start.7) | collective-permute-done | bytes 27680
  594.1 7.7 %concatenate.1 = f32[164,1728]{1,0:T(8,128)} concatenate(f32[4,1728]{1,0:T(4,128)S(1)} %collective-permute-done.7, f32[40,1728]{1,0:T(8,128)} %collective-permute-done.6, f32[40,1728]{1,0:T(8,128)} %collective-permute-done.5, f32[40,1728]{1,0:T(8,128)} %collective-permute-done.4, f32[40,1728]{1,0:T(8,128)} %get-tuple-element.32), dimensions={0} | concatenate | bytes 2267136
  602.5 1.7 constant_dynamic-slice_fusion
  604.2 20.8 %all-reduce.18.cloned.1.call-done = (f32[576,1152]{1,0:T(8,128)}, f32[576,1152]{1,0:T(8,128)}) async-done(((f32[576,1152]{1,0:T(8,128)}, f32[576,1152]{1,0:T(8,128)}), (f32[576,1152]{1,0:T(8,128)}, f32[576,1152]{1,0:T(8,128)})) %all-reduce.18.cloned.1.call-update) | async-done | bytes 5308432
  625.0 1.6 constant_dynamic-slice_fusion.3
  626.6 1.6 constant_dynamic-slice_fusion.4
  628.2 3.8 fusion.51
  632.0 48.5 %all-reduce.20.cloned.1.call-done = (f32[36,1728]{1,0:T(8,128)}, f32[18,1152]{1,0:T(8,128)}, f32[36,1728]{1,0:T(8,128)}, f32[18,1152]{1,0:T(8,128)}) async-done(((f32[36,1728]{1,0:T(8,128)}, f32[18,1152]{1,0:T(8,128)}, f32[36,1728]{1,0:T(8,128)}, f32[18,1152]{1,0:T(8,128)}), (f32[36,1728]{1,0:T(8,128)}, f32[18,1152]{1,0:T(8,128)}, f32[36,1728]{1,0:T(8,128)}, ...) | async-done | bytes 663568 | tf_op jit(solution)/shard_map/psum | solution.py:154
  680.5 1.7 broadcast_multiply_fusion.1
  682.2 1.6 broadcast_multiply_fusion.3
  683.7 1.6 broadcast_multiply_fusion.2
  685.3 1.7 broadcast_multiply_fusion
  (209 shorter events, 48.4 us)
Async XLA Ops:
  7.2 21.3 %copy-start = (bf16[576,1152]{1,0:T(8,128)(2,1)S(1)}, bf16[576,1152]{1,0:T(8,128)(2,1)}, u32[]{:S(2)}) copy-start(bf16[576,1152]{1,0:T(8,128)(2,1)} %param.15) | copy-start | bytes 3981316
  7.2 6.9 copy-start.7
  10.9 2.6 copy-start.45
  11.7 1.9 copy-start.61
  13.5 14.2 %copy-start.35 = (f32[1152]{0:T(1024)}, f32[1152]{0:T(1024)S(1)}, u32[]{:S(2)}) copy-start(f32[1152]{0:T(1024)S(1)} %get-tuple-element.16) | copy-start | bytes 13828
  13.5 14.2 %copy-start.37 = (f32[1152]{0:T(1024)}, f32[1152]{0:T(1024)S(1)}, u32[]{:S(2)}) copy-start(f32[1152]{0:T(1024)S(1)} %get-tuple-element.20) | copy-start | bytes 13828
  18.9 6.8 copy-start.13
  19.8 2.1 copy-start.1
  21.9 3.8 copy-start.30
  25.8 2.7 copy-start.62
  38.3 14.5 %copy-start.63 = (pred[384]{0:T(512)(128)(4,1)S(1)}, pred[384]{0:T(512)(128)(4,1)}, u32[]{:S(2)}) copy-start(pred[384]{0:T(512)(128)(4,1)} %copy-done.61) | copy-start | bytes 1156
  38.3 15.2 %copy-start.43 = (s32[1,32,384]{2,1,0:T(8,128)S(1)}, s32[1,32,384]{2,1,0:T(8,128)}, u32[]{:S(2)}) copy-start(s32[1,32,384]{2,1,0:T(8,128)} %param.11) | copy-start | bytes 147460
  41.3 28.6 %all-to-all-start.1 = ((bf16[32,2,6912]{2,1,0:T(2,128)(2,1)}), bf16[32,2,6912]{2,1,0:T(2,128)(2,1)}, u32[]{:S(2)}, u32[]{:S(2)}) async-start(bf16[32,2,6912]{2,1,0:T(2,128)(2,1)} %reshape.894), calls=%async_computation.1 | async-start | bytes 1769472 | tf_op jit(solution)/shard_map/all_to_all | solution.py:139
  64.4 3.0 copy-start.66
  64.4 4.9 copy-start.31
  69.9 27.8 %all-to-all-start = ((bf16[32,2,6912]{2,1,0:T(2,128)(2,1)}), bf16[32,2,6912]{2,1,0:T(2,128)(2,1)}, u32[]{:S(2)}, u32[]{:S(2)}) async-start(bf16[32,2,6912]{2,1,0:T(2,128)(2,1)} %reshape.896), calls=%async_computation | async-start | bytes 1769472 | tf_op jit(solution)/shard_map/all_to_all | solution.py:140
  141.9 2.0 copy-start.17
  141.9 2.0 copy-start.18
  151.4 1.8 copy-start.39
  151.4 1.8 copy-start.40
  151.4 1.8 copy-start.59
  163.6 2.9 copy-start.16
  166.9 4.3 copy-start.21
  169.7 2.4 copy-start.41
  169.7 2.4 copy-start.42
  169.7 2.4 copy-start.55
  169.7 2.4 copy-start.58
  169.8 2.4 copy-start.60
  172.1 5.8 copy-start.24
  172.1 5.8 copy-start.4
  172.1 5.8 copy-start.6
  181.7 9.7 %copy-start.20 = (bf16[32,12,1152]{2,1,0:T(8,128)(2,1)S(1)}, bf16[32,12,1152]{2,1,0:T(8,128)(2,1)}, u32[]{:S(2)}) copy-start(bf16[32,12,1152]{2,1,0:T(8,128)(2,1)} %convert_element_type.372) | copy-start | bytes 2654212
  181.7 40.7 %all-to-all-start.2 = ((f32[32,12,1152]{2,1,0:T(8,128)}), f32[32,12,1152]{2,1,0:T(8,128)}, u32[]{:S(2)}, u32[]{:S(2)}) async-start(f32[32,12,1152]{2,1,0:T(8,128)} %copy.111), calls=%async_computation.2 | async-start | bytes 4718592 | tf_op jit(solution)/shard_map/all_to_all | solution.py:146
  191.3 3.8 copy-start.22
  191.3 3.7 copy-start.56
  191.3 3.7 copy-start.57
  191.3 433.7 %all-reduce.18.cloned.1.call-start = ((), (), s32[]{:S(2)}) async-start(), calls=%async_computation.3 | async-start | bytes 10616832
  191.4 3.7 copy-start.5
  191.4 3.7 copy-start.23
  191.4 3.7 copy-start.25
  201.1 24.1 %copy-start.36 = (f32[1152]{0:T(1024)S(1)}, f32[1152]{0:T(1024)}, u32[]{:S(2)}) copy-start(f32[1152]{0:T(1024)} %copy-done.35) | copy-start | bytes 13828
  201.1 24.1 %copy-start.38 = (f32[1152]{0:T(1024)S(1)}, f32[1152]{0:T(1024)}, u32[]{:S(2)}) copy-start(f32[1152]{0:T(1024)} %copy-done.37) | copy-start | bytes 13828
  201.1 24.1 %copy-start.64 = (pred[384]{0:T(512)(128)(4,1)S(1)}, pred[384]{0:T(512)(128)(4,1)}, u32[]{:S(2)}) copy-start(pred[384]{0:T(512)(128)(4,1)} %copy-done.61) | copy-start | bytes 1156
  222.4 9.9 %slice-start = ((s8[4718592]{0:T(1024)(128)(4,1)}), s8[524288]{0:T(1024)(128)(4,1)S(1)}, s32[]{:S(2)}) async-start(s8[4718592]{0:T(1024)(128)(4,1)} %bitcast.236), calls=%async_computation.5 | async-start | bytes 1048576
  225.2 7.0 %slice-start.1 = ((s8[4718592]{0:T(1024)(128)(4,1)}), s8[4194304]{0:T(1024)(128)(4,1)S(1)}, s32[]{:S(2)}) async-start(s8[4718592]{0:T(1024)(128)(4,1)} %bitcast.236), calls=%async_computation.6 | async-start | bytes 8388608
  227.8 3.6 copy-start.14
  233.6 1.5 copy-start.34
  233.6 1.5 copy-start.3
  233.7 1.5 copy-start.12
  237.1 2.0 copy-start.44
  244.6 1.4 copy-start.27
  244.6 1.4 copy-start.46
  244.7 435.8 %all-reduce.20.cloned.1.call-start = ((), (), s32[]{:S(2)}) async-start(), calls=%async_computation.4 | async-start | bytes 1589248 | tf_op jit(solution)/shard_map/psum | solution.py:154
  536.0 14.1 %copy-start.19 = (f32[40,1728]{1,0:T(8,128)}, f32[40,1728]{1,0:T(8,128)S(1)}, u32[]{:S(2)}) copy-start(f32[40,1728]{1,0:T(8,128)S(1)} %get-tuple-element.31) | copy-start | bytes 829444
  536.1 29.1 %collective-permute-start.2 = (f32[40,1728]{1,0:T(8,128)S(1)}, f32[40,1728]{1,0:T(8,128)S(1)}, u32[]{:S(2)}, u32[]{:S(2)}) collective-permute-start(f32[40,1728]{1,0:T(8,128)S(1)} %get-tuple-element.31), channel_id=1, source_target_pairs={{0,12},{4,16},{8,20},{12,24},{16,28},{20,32},{24,36},{28,40},{32,4... | collective-permute-start | bytes 829448
  537.4 35.5 %collective-permute-start.1 = (f32[40,1728]{1,0:T(8,128)S(1)}, f32[40,1728]{1,0:T(8,128)S(1)}, u32[]{:S(2)}, u32[]{:S(2)}) collective-permute-start(f32[40,1728]{1,0:T(8,128)S(1)} %get-tuple-element.31), channel_id=1, source_target_pairs={{0,8},{4,12},{8,16},{12,20},{16,24},{20,28},{24,32},{28,36},{32,40... | collective-permute-start | bytes 829448
  540.0 20.6 %collective-permute-start.3 = (f32[4,1728]{1,0:T(4,128)S(1)}, f32[4,1728]{1,0:T(4,128)S(1)}, u32[]{:S(2)}, u32[]{:S(2)}) collective-permute-start(f32[4,1728]{1,0:T(4,128)S(1)} %slice.103), channel_id=1, source_target_pairs={{0,16},{4,20},{8,24},{12,28},{16,32},{20,36},{24,40},{28,44},{32,4... | collective-permute-start | bytes 82952
  550.1 27.1 %collective-permute-start = (f32[40,1728]{1,0:T(8,128)S(1)}, f32[40,1728]{1,0:T(8,128)}, u32[]{:S(2)}, u32[]{:S(2)}) collective-permute-start(f32[40,1728]{1,0:T(8,128)S(1)} %get-tuple-element.31), channel_id=1, source_target_pairs={{0,4},{4,8},{8,12},{12,16},{16,20},{20,24},{24,28},{28,32},{32,36}... | collective-permute-start | bytes 829448
  554.3 39.8 %collective-permute-start.6 = (f32[40,1728]{1,0:T(8,128)}, f32[40,1728]{1,0:T(8,128)}, u32[]{:S(2)}, u32[]{:S(2)}) collective-permute-start(f32[40,1728]{1,0:T(8,128)} %get-tuple-element.32), channel_id=1, source_target_pairs={{0,12},{4,16},{8,20},{12,24},{16,28},{20,32},{24,36},{28,40},{32,4... | collective-permute-start | bytes 829448
  560.6 33.5 %collective-permute-start.5 = (f32[40,1728]{1,0:T(8,128)}, f32[40,1728]{1,0:T(8,128)}, u32[]{:S(2)}, u32[]{:S(2)}) collective-permute-start(f32[40,1728]{1,0:T(8,128)} %get-tuple-element.32), channel_id=1, source_target_pairs={{0,8},{4,12},{8,16},{12,20},{16,24},{20,28},{24,32},{28,36},{32,40... | collective-permute-start | bytes 829448
  565.1 12.1 %copy-start.28 = (f32[40,1728]{1,0:T(8,128)}, f32[40,1728]{1,0:T(8,128)S(1)}, u32[]{:S(2)}) copy-start(f32[40,1728]{1,0:T(8,128)S(1)} %collective-permute-done.2) | copy-start | bytes 829444
  565.1 29.0 %collective-permute-start.4 = (f32[40,1728]{1,0:T(8,128)}, f32[40,1728]{1,0:T(8,128)}, u32[]{:S(2)}, u32[]{:S(2)}) collective-permute-start(f32[40,1728]{1,0:T(8,128)} %get-tuple-element.32), channel_id=1, source_target_pairs={{0,4},{4,8},{8,12},{12,16},{16,20},{20,24},{24,28},{28,32},{32,36}... | collective-permute-start | bytes 829448
  572.9 4.3 copy-start.29
  572.9 21.2 %collective-permute-start.7 = (f32[4,1728]{1,0:T(4,128)S(1)}, f32[4,1728]{1,0:T(4,128)S(1)}, u32[]{:S(2)}, u32[]{:S(2)}) collective-permute-start(f32[4,1728]{1,0:T(4,128)S(1)} %slice.104), channel_id=1, source_target_pairs={{0,16},{4,20},{8,24},{12,28},{16,32},{20,36},{24,40},{28,44},{32,4... | collective-permute-start | bytes 82952
  (18 other events, 19.7 us)
Sparse Core Ops, SparseCore 0:
  244.8 380.1 all-reduce.17
  628.6 51.8 all-reduce.19
where the time goes:
time: 700 us; the launch traced here: 694 us
  blocking collectives  283 us (40%)
  waiting for transfers between devices  103 us (15%)
  local copies, waits for them, and re-layouts  88.6 us (13%)
  other arithmetic  68.9 us (10%)
  matrix products  67.8 us (10%)
  starting transfers between devices  65.2 us (9%)
  between operations  17.4 us (2%)
    unnamed x1, blocking collectives  283 us
    psum x1, waiting for transfers between devices, body(): summed = lax.psum((shares[0], shares[1], shares[2], shares[3]), 'dp')  48.5 us
    unnamed x152, local copies, waits for them, and re-layouts  41.1 us
    unnamed x9, starting transfers between devices  34.5 us
    unnamed x11, waiting for transfers between devices  33.4 us
    all_to_all x1, waiting for transfers between devices, body(): lax.all_to_all(dmiddle_patch, 'seq', split_axis=0, concat_axis=1, tiled=T...  21.3 us
  transfers between devices with their start and end apart: 13, of which 4 were waited for; matrix products, arithmetic and copies ran while one was open for 52% of the time, Pallas kernels for 0%

commit v1 on v0

--- a/solution.py
+++ b/solution.py
@@ -143,22 +143,32 @@
         middle_patch, patch_marks, row_clean, row_noised, 3, wqkv_t, wo_t, core_temporal
     )
     dmiddle_patch, gq_t, go_t = branch_backward(saved_t, wqkv_t, wo_t, core_temporal, dpatch)
-    dmiddle = lax.all_to_all(dmiddle_patch, "seq", split_axis=0, concat_axis=1, tiled=True)
+    dmiddle = lax.all_to_all(
+        dmiddle_patch.astype(jnp.bfloat16), "seq", split_axis=0, concat_axis=1, tiled=True
+    )
     dlocal, gq_s, go_s = branch_backward(saved_s, wqkv_s, wo_s, core_spatial, dmiddle)
-    shares = (
-        lax.psum_scatter(gq_s, "seq", scatter_dimension=0, tiled=True),
-        lax.psum_scatter(go_s, "seq", scatter_dimension=0, tiled=True),
-        lax.psum_scatter(gq_t, "seq", scatter_dimension=0, tiled=True),
-        lax.psum_scatter(go_t, "seq", scatter_dimension=0, tiled=True),
+    factor = 1.0 / math.sqrt(lax.axis_size("dp") * frame_count * seq_count * patches)
+    gq_t, go_t = reduce_pair(gq_t, go_t, factor)
+    gq_s, go_s = reduce_pair(gq_s, go_s, factor)
+    return (dlocal[None], gq_s, go_s, gq_t, go_t)
+
+
+def reduce_pair(gq, go, factor):
+    count = lax.axis_size("seq")
+    packed = jnp.concatenate(
+        [
+            gq.astype(jnp.bfloat16).reshape(count, -1, 128),
+            go.astype(jnp.bfloat16).reshape(count, -1, 128),
+        ],
+        axis=1,
     )
-    summed = lax.psum((shares[0], shares[1], shares[2], shares[3]), "dp")
-    factor = 1.0 / math.sqrt(lax.axis_size("dp") * frame_count * seq_count * patches)
+    shares = lax.all_to_all(packed, "seq", 0, 0, tiled=True)
+    own = jnp.sum(shares.astype(jnp.float32), axis=0)
+    total = jnp.sum(lax.all_gather(own, "dp", axis=0), axis=0) * factor
+    cut = gq.size // count // 128
     return (
-        dlocal[None],
-        summed[0] * factor,
-        summed[1] * factor,
-        summed[2] * factor,
-        summed[3] * factor,
+        total[:cut].reshape(gq.shape[0] // count, gq.shape[1]),
+        total[cut:].reshape(go.shape[0] // count, go.shape[1]),
     )
 
 

time: 700 us -> 434 us (0.62)
  blocking collectives: 283 us -> 0 us
  local copies, waits for them, and re-layouts: 88.6 us -> 107 us
  other arithmetic: 68.9 us -> 83.9 us
  starting transfers between devices: 65.2 us -> 51.7 us
  matrix products: 67.8 us -> 60.3 us
    unnamed x1 -> x0, blocking collectives: 283 us -> none
    all_to_all x1 -> x3, waiting for transfers between devices: 21.3 us -> 85.2 us  [the longest x2 85.2 us: reduce_pair(): shares = lax.all_to_all(packed, 'seq', 0, 0, tiled=True)]
    psum x1 -> x0, waiting for transfers between devices: 48.5 us -> none  [body(): summed = lax.psum((shares[0], shares[1], shares[2], shares[3]), 'dp')]
    unnamed x9 -> x0, starting transfers between devices: 34.5 us -> none
    unnamed x11 -> x2, waiting for transfers between devices: 33.4 us -> 0.03 us
    reshape x0 -> x8, local copies, waits for them, and re-layouts: none -> 26.4 us  [the longest x2 16.5 us: reduce_pair(): gq.astype(jnp.bfloat16).reshape(count, -1, 128)]
    all_gather x0 -> x2, waiting for transfers between devices: none -> 22.6 us  [reduce_pair(): total = jnp.sum(lax.all_gather(own, 'dp', axis=0), axis=0) * factor]
    all_to_all x1 -> x3, starting transfers between devices: 9.59 us -> 30.8 us  [the longest x2 21 us: reduce_pair(): shares = lax.all_to_all(packed, 'seq', 0, 0, tiled=True)]
  transfers between devices with their start and end apart: 13 -> 7, of which waited for: 4 -> 4; matrix products, arithmetic and copies ran while one was open for 52% -> 31% of each run, Pallas kernels for 0% -> 0%
where the time goes in v1:
time: 434 us; the launch traced here: 427 us
  waiting for transfers between devices  108 us (25%)
  local copies, waits for them, and re-layouts  107 us (25%)
  other arithmetic  83.9 us (19%)
  matrix products  60.3 us (14%)
  starting transfers between devices  51.7 us (12%)
  between operations  16.1 us (4%)
    all_to_all x2, waiting for transfers between devices, reduce_pair(): shares = lax.all_to_all(packed, 'seq', 0, 0, tiled=True)  85.2 us
    all_gather x2, waiting for transfers between devices, reduce_pair(): total = jnp.sum(lax.all_gather(own, 'dp', axis=0), axis=0) * factor  22.6 us
    unnamed x129, local copies, waits for them, and re-layouts  21.1 us
    all_to_all x2, starting transfers between devices, reduce_pair(): shares = lax.all_to_all(packed, 'seq', 0, 0, tiled=True)  21 us
    reshape x2, local copies, waits for them, and re-layouts, reduce_pair(): gq.astype(jnp.bfloat16).reshape(count, -1, 128)  16.5 us
    unnamed x3, other arithmetic  13.9 us
    convert_element_type x2, local copies, waits for them, and re-layouts, reduce_pair(): gq.astype(jnp.bfloat16).reshape(count, -1, 128)  13.1 us
    all_to_all x1, starting transfers between devices, body(): lax.all_to_all(middle, 'seq', split_axis=1, concat_axis=0, tiled=True)  11.5 us
  transfers between devices with their start and end apart: 7, of which 4 were waited for; matrix products, arithmetic and copies ran while one was open for 31% of the time, Pallas kernels for 0%

profile of v1, /device:TPU:1, one launch (start us, length us, event | category | flops | bytes accessed | tf_op | source)
XLA Modules:
  0.0 427.1 jit_solution(16377223892095175324)
XLA Ops:
  9.4 1.5 fusion.55
  11.7 1.8 slice_reduce_fusion.2
  14.1 4.7 %fusion.26 = bf16[1,384,1728]{1,2,0:T(8,128)(2,1)S(1)} fusion(bf16[1152,1728]{0,1:T(8,128)(2,1)} %param.14, bf16[1,1,384,1152]{3,2,1,0:T(8,128)(2,1)S(1)} %copy-done.7, f32[1152]{0:T(1024)S(1)} %get-tuple-element.14, f32[1152]{0:T(1024)S(1)} %get-tuple-element.17, f32[1152]{0:T(1024)S(1)} %get-tuple-element.15, f32[1152]{0:T(1024)S(1)} %get-tuple-element.18, ...), kind=kOutput, calls=%fused_computation.44 | convolution fusion | flops 1533468672 | bytes 6215040 | tf_op jit(solution)/shard_map/dot_general | solution.py:60
  20.6 1.4 copy-done.1
  22.0 3.5 convert_reduce_fusion.2
  25.5 1.4 copy-done.2
  31.1 6.9 %reduce.50 = bf16[384,1152]{1,0:T(8,128)(2,1)} reduce(bf16[384,1,1152]{2,1,0:T(2,128)(2,1)S(1)} %bitcast.238, bf16[]{:T(256)} %broadcast.590), dimensions={1}, to_apply=%bitcast.231.reduce_sub_computation | reduce | bytes 1769474
  38.1 2.9 reshape.935
  41.0 11.5 %all-to-all-start.1 = ((bf16[32,2,6912]{2,1,0:T(2,128)(2,1)}), bf16[32,2,6912]{2,1,0:T(2,128)(2,1)}, u32[]{:S(2)}, u32[]{:S(2)}) async-start(bf16[32,2,6912]{2,1,0:T(2,128)(2,1)} %reshape.935), calls=%async_computation.1 | async-start | bytes 1769472 | tf_op jit(solution)/shard_map/all_to_all | solution.py:139
  54.1 2.5 copy.211
  56.6 6.9 %reduce.51 = bf16[384,1152]{1,0:T(8,128)(2,1)} reduce(bf16[384,1,1152]{2,1,0:T(2,128)(2,1)S(1)} %bitcast.239, bf16[]{:T(256)} %broadcast.590), dimensions={1}, to_apply=%bitcast.232.reduce_sub_computation | reduce | bytes 1769474
  63.5 2.9 reshape.937
  67.0 9.4 %all-to-all-start = ((bf16[32,2,6912]{2,1,0:T(2,128)(2,1)}), bf16[32,2,6912]{2,1,0:T(2,128)(2,1)}, u32[]{:S(2)}, u32[]{:S(2)}) async-start(bf16[32,2,6912]{2,1,0:T(2,128)(2,1)} %reshape.937), calls=%async_computation | async-start | bytes 1769472 | tf_op jit(solution)/shard_map/all_to_all | solution.py:140
  76.4 5.0 %reshape.936 = bf16[384,1,1152]{2,1,0:T(2,128)(2,1)S(1)} reshape(bf16[32,2,6912]{2,1,0:T(2,128)(2,1)} %all-to-all-done.1) | data formatting | bytes 1769472
  81.4 1.9 convert_reduce_fusion.7
  83.9 1.4 div.96
  85.3 9.2 %convert_reduce_fusion.6 = (f32[384,1152]{1,0:T(8,128)}, f32[384]{0:T(512)}) fusion(f32[384]{0:T(512)} %broadcast_multiply_fusion.6, bf16[384,1,1152]{2,1,0:T(2,128)(2,1)S(1)} %reshape.936), kind=kLoop, calls=%fused_computation.94 | loop fusion | flops 1769088 | bytes 2657280 | tf_op jit(solution)/shard_map/convert_element_type | solution.py:53
  94.5 5.0 %reshape.938 = bf16[384,1,1152]{2,1,0:T(2,128)(2,1)S(1)} reshape(bf16[32,2,6912]{2,1,0:T(2,128)(2,1)} %all-to-all-done) | data formatting | bytes 1769472
  99.5 6.3 %convert_reduce_fusion.4 = f32[384,1152]{1,0:T(8,128)} fusion(bf16[384,1,1152]{2,1,0:T(2,128)(2,1)S(1)} %reshape.938), kind=kLoop, calls=%fused_computation.86 | loop fusion | flops 442368 | bytes 2654208 | tf_op jit(solution)/shard_map/convert_element_type | solution.py:90
  105.8 2.9 reshape.907
  108.7 4.1 fusion.74
  112.7 2.6 reshape.891
  120.8 2.8 reshape.909
  123.6 5.4 %fusion.22 = bf16[32,12,1728]{2,0,1:T(8,128)(2,1)S(1)} fusion(bf16[1152,1728]{0,1:T(8,128)(2,1)} %param.16, f32[1152]{0:T(1024)} %get-tuple-element.19, f32[1152]{0:T(1024)} %get-tuple-element.21, f32[1152]{0:T(1024)} %get-tuple-element.12, f32[1152]{0:T(1024)} %get-tuple-element.22, pred[32,12]{0,1:T(8,128)(4,1)} %copy.130, f32[32,12]{0,1:T(8,128)} %copy.129, ...), kind=kOutput, calls=%fused_computation.41 | convolution fusion | flops 1533026304 | bytes 7099776 | tf_op jit(solution)/shard_map/dot_general | solution.py:60
  130.4 2.6 reshape.894
  133.0 2.6 reshape.893
  135.6 2.8 reshape.892
  138.4 2.0 convolution_convert_fusion.6
  146.1 1.8 fusion.73
  147.9 1.8 fusion.72
  149.7 8.2 %convert_reduce_fusion.5 = bf16[384,1152]{1,0:T(8,128)(2,1)} fusion(pred[384]{0:T(512)(128)(4,1)S(1)} %copy-done.53, f32[1152]{0:T(1024)S(1)} %copy-done.35, f32[1152]{0:T(1024)S(1)} %copy-done.34, bf16[384,1,1152]{2,1,0:T(2,128)(2,1)S(1)} %reshape.938), kind=kLoop, calls=%fused_computation.87 | loop fusion | flops 1769472 | bytes 1779072 | tf_op jit(solution)/shard_map/convert_element_type | solution.py:91
  157.9 2.4 convert_element_type.416
  160.3 1.5 copy.137
  163.5 1.4 convert_element_type.413
  164.9 1.4 copy.141
  168.8 5.8 %fusion.151 = (f32[32,12]{0,1:T(8,128)S(1)}, f32[32,12]{0,1:T(8,128)S(1)}, f32[32,12,1152]{2,0,1:T(8,128)S(1)}) fusion(f32[32,12]{0,1:T(8,128)S(1)} %copy-done.36, f32[32,12]{0,1:T(8,128)S(1)} %copy-done.37, f32[32,12,1152]{2,1,0:T(8,128)} %reshape.909, f32[1152]{0:T(1024)S(1)} %copy-done.49, f32[1152]{0:T(1024)S(1)} %copy-done.52, ...), kind=kOutput, calls=%fused_computation.214 | convolution fusion | flops 1536343296 | bytes 8863104 | tf_op jit(solution)/shard_map/dot_general | solution.py:111
  177.2 9.8 %all-to-all-start.2 = ((bf16[32,12,1152]{2,1,0:T(8,128)(2,1)}), bf16[32,12,1152]{2,1,0:T(8,128)(2,1)S(1)}, u32[]{:S(2)}, u32[]{:S(2)}) async-start(bf16[32,12,1152]{2,1,0:T(8,128)(2,1)} %copy.146), calls=%async_computation.2 | async-start | bytes 2359296 | tf_op jit(solution)/shard_map/all_to_all | solution.py:146
  187.1 3.3 fusion.20
  190.4 3.5 reshape.904
  193.8 6.8 %fusion = bf16[1152,1728]{0,1:T(8,128)(2,1)} fusion(bf16[32,12,576]{2,0,1:T(8,128)(2,1)} %copy-done.23, bf16[32,12,576]{2,0,1:T(8,128)(2,1)} %convert_element_type.375, bf16[32,12,576]{2,0,1:T(8,128)(2,1)S(1)} %copy-done.22, f32[1152]{0:T(1024)S(1)} %copy-done.50, f32[1152]{0:T(1024)S(1)} %copy-done.51, f32[1152]{0:T(1024)S(1)} %copy-done.49, ...), kind=kOutput, calls=%fused_computation.3 | convolution fusion | flops 1538334720 | bytes 7099776 | tf_op jit(solution)/shard_map/dot_general | solution.py:105
  200.7 6.4 %copy.152 = bf16[1152,1728]{1,0:T(8,128)(2,1)} copy(bf16[1152,1728]{0,1:T(8,128)(2,1)} %fusion) | data formatting | bytes 7962624 | tf_op jit(solution)/shard_map/convert_element_type | solution.py:160
  207.1 8.2 %reshape.903 = bf16[32,486,128]{2,1,0:T(8,128)(2,1)} reshape(bf16[1152,1728]{1,0:T(8,128)(2,1)} %copy.152) | data formatting | bytes 7962624 | tf_op jit(solution)/shard_map/reshape | solution.py:160
  215.4 5.6 %pad_maximum_fusion.1 = bf16[32,648,128]{2,1,0:T(8,128)(2,1)} fusion(bf16[32,162,128]{2,1,0:T(8,128)(2,1)} %reshape.904, bf16[32,486,128]{2,1,0:T(8,128)(2,1)} %reshape.903), kind=kLoop, calls=%fused_computation.8 | loop fusion | flops 10616832 | bytes 10616832 | tf_op jit(solution)/shard_map/concatenate | solution.py:158
  221.0 9.8 %all-to-all-start.4 = ((bf16[32,648,128]{2,1,0:T(8,128)(2,1)}), bf16[32,648,128]{2,1,0:T(8,128)(2,1)}, u32[]{:S(2)}, u32[]{:S(2)}) async-start(bf16[32,648,128]{2,1,0:T(8,128)(2,1)} %pad_maximum_fusion.1), calls=%async_computation.4 | async-start | bytes 10616832 | tf_op jit(solution)/shard_map/all_to_all | solution.py:165
  232.3 2.2 convert_element_type.407
  234.5 3.1 convolution_convert_fusion.1
  237.6 3.4 reshape.900
  242.4 2.5 convolution_convert_fusion.8
  245.8 4.1 fusion.4
  249.9 1.5 fusion.152
  255.2 4.5 %convolution_convert_fusion = bf16[1152,1728]{0,1:T(8,128)(2,1)} fusion(bf16[1,1,384,1152]{3,2,1,0:T(8,128)(2,1)S(1)} %copy-done.8, f32[1152]{0:T(1024)S(1)} %copy-done.46, f32[1152]{0:T(1024)S(1)} %copy-done.48, f32[1152]{0:T(1024)S(1)} %copy-done.42, f32[1152]{0:T(1024)S(1)} %copy-done.44, f32[384]{0:T(512)S(1)} %copy-done.40, ...), kind=kOutput, calls=%fused_computation.4 | convolution fusion | flops 1538777088 | bytes 6215040 | tf_op jit(solution)/shard_map/dot_general | solution.py:105
  259.7 6.6 %copy.151 = bf16[1152,1728]{1,0:T(8,128)(2,1)} copy(bf16[1152,1728]{0,1:T(8,128)(2,1)} %convolution_convert_fusion) | data formatting | bytes 7962624 | tf_op jit(solution)/shard_map/convert_element_type | solution.py:160
  266.4 8.3 %reshape.899 = bf16[32,486,128]{2,1,0:T(8,128)(2,1)} reshape(bf16[1152,1728]{1,0:T(8,128)(2,1)} %copy.151) | data formatting | bytes 7962624 | tf_op jit(solution)/shard_map/reshape | solution.py:160
  274.6 5.6 %pad_maximum_fusion = bf16[32,648,128]{2,1,0:T(8,128)(2,1)} fusion(bf16[32,162,128]{2,1,0:T(8,128)(2,1)} %reshape.900, bf16[32,486,128]{2,1,0:T(8,128)(2,1)} %reshape.899), kind=kLoop, calls=%fused_computation.7 | loop fusion | flops 10616832 | bytes 10616832 | tf_op jit(solution)/shard_map/concatenate | solution.py:158
  280.3 20.6 %all-to-all-done.4 = bf16[32,648,128]{2,1,0:T(8,128)(2,1)} async-done(((bf16[32,648,128]{2,1,0:T(8,128)(2,1)}), bf16[32,648,128]{2,1,0:T(8,128)(2,1)}, u32[]{:S(2)}, u32[]{:S(2)}) %all-to-all-start.4) | async-done | bytes 5308448 | tf_op jit(solution)/shard_map/all_to_all | solution.py:165
  300.8 11.2 %all-to-all-start.3 = ((bf16[32,648,128]{2,1,0:T(8,128)(2,1)}), bf16[32,648,128]{2,1,0:T(8,128)(2,1)}, u32[]{:S(2)}, u32[]{:S(2)}) async-start(bf16[32,648,128]{2,1,0:T(8,128)(2,1)} %pad_maximum_fusion), calls=%async_computation.3 | async-start | bytes 10616832 | tf_op jit(solution)/shard_map/all_to_all | solution.py:165
  312.1 4.0 convert_reduce_fusion
  316.2 64.6 %all-to-all-done.3 = bf16[32,648,128]{2,1,0:T(8,128)(2,1)} async-done(((bf16[32,648,128]{2,1,0:T(8,128)(2,1)}), bf16[32,648,128]{2,1,0:T(8,128)(2,1)}, u32[]{:S(2)}, u32[]{:S(2)}) %all-to-all-start.3) | async-done | bytes 5308448 | tf_op jit(solution)/shard_map/all_to_all | solution.py:165
  380.8 4.0 convert_reduce_fusion.1
  384.9 4.8 %fusion.150 = (f32[384]{0:T(512)S(1)}, f32[384]{0:T(512)S(1)}, f32[384,1152]{1,0:T(8,128)S(1)}) fusion(f32[384]{0:T(512)S(1)} %copy-done.40, f32[384]{0:T(512)S(1)} %broadcast_multiply_fusion.7, bf16[1,1,384,1152]{3,2,1,0:T(8,128)(2,1)S(1)} %copy-done.8, f32[1152]{0:T(1024)S(1)} %copy-done.42, f32[1152]{0:T(1024)} %copy-done.43, ...), kind=kOutput, calls=%fused_computation.213 | convolution fusion | flops 1536785664 | bytes 7978368 | tf_op jit(solution)/shard_map/dot_general | solution.py:111
  389.7 1.8 fusion.51
  391.5 1.4 reduce_sum.223
  394.5 22.6 %all-gather.5.cloned.1.call-done = f32[2592,128]{1,0:T(8,128)} async-done(((f32[648,128]{1,0:T(8,128)}), f32[2592,128]{1,0:T(8,128)}) %all-gather.5.cloned.1.call-update) | async-done | bytes 1327120 | tf_op jit(solution)/shard_map/all_gather | solution.py:167
  417.1 1.4 reduce_sum.221
  (191 shorter events, 41.0 us)
Async XLA Ops:
  7.2 21.0 %copy-start = (bf16[576,1152]{1,0:T(8,128)(2,1)S(1)}, bf16[576,1152]{1,0:T(8,128)(2,1)}, u32[]{:S(2)}) copy-start(bf16[576,1152]{1,0:T(8,128)(2,1)} %param.15) | copy-start | bytes 3981316
  7.2 6.9 %copy-start.7 = (bf16[1,1,384,1152]{3,2,1,0:T(8,128)(2,1)S(1)}, bf16[1,1,384,1152]{3,2,1,0:T(8,128)(2,1)}, u32[]{:S(2)}) copy-start(bf16[1,1,384,1152]{3,2,1,0:T(8,128)(2,1)} %param.9) | copy-start | bytes 2654212
  10.9 2.6 copy-start.39
  11.7 1.8 copy-start.56
  13.5 13.9 %copy-start.30 = (f32[1152]{0:T(1024)}, f32[1152]{0:T(1024)S(1)}, u32[]{:S(2)}) copy-start(f32[1152]{0:T(1024)S(1)} %get-tuple-element.16) | copy-start | bytes 13828
  13.5 13.9 %copy-start.32 = (f32[1152]{0:T(1024)}, f32[1152]{0:T(1024)S(1)}, u32[]{:S(2)}) copy-start(f32[1152]{0:T(1024)S(1)} %get-tuple-element.20) | copy-start | bytes 13828
  18.9 0.9 copy-start.12
  18.9 6.5 %copy-start.14 = (bf16[1,384,576]{1,2,0:T(8,128)(2,1)}, bf16[1,384,576]{1,2,0:T(8,128)(2,1)S(1)}, u32[]{:S(2)}) copy-start(bf16[1,384,576]{1,2,0:T(8,128)(2,1)S(1)} %get-tuple-element.39) | copy-start | bytes 1327108
  19.8 2.2 copy-start.1
  22.0 3.5 copy-start.27
  25.5 1.4 copy-start.2
  25.5 2.8 copy-start.57
  38.1 14.5 %copy-start.38 = (s32[1,32,384]{2,1,0:T(8,128)S(1)}, s32[1,32,384]{2,1,0:T(8,128)}, u32[]{:S(2)}) copy-start(s32[1,32,384]{2,1,0:T(8,128)} %param.11) | copy-start | bytes 147460
  41.0 26.0 %all-to-all-start.1 = ((bf16[32,2,6912]{2,1,0:T(2,128)(2,1)}), bf16[32,2,6912]{2,1,0:T(2,128)(2,1)}, u32[]{:S(2)}, u32[]{:S(2)}) async-start(bf16[32,2,6912]{2,1,0:T(2,128)(2,1)} %reshape.935), calls=%async_computation.1 | async-start | bytes 1769472 | tf_op jit(solution)/shard_map/all_to_all | solution.py:139
  67.0 27.5 %all-to-all-start = ((bf16[32,2,6912]{2,1,0:T(2,128)(2,1)}), bf16[32,2,6912]{2,1,0:T(2,128)(2,1)}, u32[]{:S(2)}, u32[]{:S(2)}) async-start(bf16[32,2,6912]{2,1,0:T(2,128)(2,1)} %reshape.937), calls=%async_computation | async-start | bytes 1769472 | tf_op jit(solution)/shard_map/all_to_all | solution.py:140
  138.4 2.0 copy-start.17
  138.4 2.0 copy-start.18
  142.1 1.3 copy-start.11
  143.5 1.3 copy-start.10
  147.9 1.8 copy-start.34
  147.9 1.8 copy-start.35
  147.9 1.8 copy-start.53
  160.3 2.9 copy-start.16
  163.5 4.3 %copy-start.21 = (bf16[32,12,8,72]{3,0,2,1:T(8,128)(2,1)S(1)}, bf16[32,12,8,72]{3,0,2,1:T(8,128)(2,1)}, u32[]{:S(2)}) copy-start(bf16[32,12,8,72]{3,0,2,1:T(8,128)(2,1)} %fusion.73) | copy-start | bytes 1327108
  166.4 2.3 copy-start.36
  166.4 2.3 copy-start.37
  166.4 2.3 copy-start.49
  166.4 2.3 copy-start.52
  166.4 2.3 copy-start.54
  168.8 5.8 %copy-start.23 = (bf16[32,12,576]{2,0,1:T(8,128)(2,1)}, bf16[32,12,576]{2,0,1:T(8,128)(2,1)S(1)}, u32[]{:S(2)}) copy-start(bf16[32,12,576]{2,0,1:T(8,128)(2,1)S(1)} %convert_element_type.378) | copy-start | bytes 1327108
  168.8 5.8 %copy-start.5 = (f32[32,12,1152]{2,1,0:T(8,128)S(1)}, f32[32,12,1152]{2,1,0:T(8,128)}, u32[]{:S(2)}) copy-start(f32[32,12,1152]{2,1,0:T(8,128)} %reshape.909) | copy-start | bytes 5308420
  168.8 5.8 %copy-start.6 = (f32[32,12,1152]{2,1,0:T(8,128)S(1)}, f32[32,12,1152]{2,1,0:T(8,128)}, u32[]{:S(2)}) copy-start(f32[32,12,1152]{2,1,0:T(8,128)} %reshape.907) | copy-start | bytes 5308420
  175.9 11.2 %copy-start.24 = (bf16[32,12,576]{2,0,1:T(8,128)(2,1)S(1)}, bf16[32,12,576]{2,0,1:T(8,128)(2,1)}, u32[]{:S(2)}) copy-start(bf16[32,12,576]{2,0,1:T(8,128)(2,1)} %convert_element_type.413) | copy-start | bytes 1327108
  177.2 43.7 %all-to-all-start.2 = ((bf16[32,12,1152]{2,1,0:T(8,128)(2,1)}), bf16[32,12,1152]{2,1,0:T(8,128)(2,1)S(1)}, u32[]{:S(2)}, u32[]{:S(2)}) async-start(bf16[32,12,1152]{2,1,0:T(8,128)(2,1)} %copy.146), calls=%async_computation.2 | async-start | bytes 2359296 | tf_op jit(solution)/shard_map/all_to_all | solution.py:146
  190.3 3.5 copy-start.22
  190.3 3.5 copy-start.50
  190.4 3.5 copy-start.51
  190.4 3.5 copy-start.55
  221.0 9.8 %copy-start.58 = (pred[384]{0:T(512)(128)(4,1)S(1)}, pred[384]{0:T(512)(128)(4,1)}, u32[]{:S(2)}) copy-start(pred[384]{0:T(512)(128)(4,1)} %copy-done.56) | copy-start | bytes 1156
  221.0 9.9 %copy-start.28 = (f32[8,384]{1,0:T(8,128)S(1)}, f32[8,384]{1,0:T(8,128)}, u32[]{:S(2)}) copy-start(f32[8,384]{1,0:T(8,128)} %copy-done.27) | copy-start | bytes 36868
  221.0 10.0 %copy-start.31 = (f32[1152]{0:T(1024)S(1)}, f32[1152]{0:T(1024)}, u32[]{:S(2)}) copy-start(f32[1152]{0:T(1024)} %copy-done.30) | copy-start | bytes 13828
  221.0 10.0 %copy-start.33 = (f32[1152]{0:T(1024)S(1)}, f32[1152]{0:T(1024)}, u32[]{:S(2)}) copy-start(f32[1152]{0:T(1024)} %copy-done.32) | copy-start | bytes 13828
  221.0 79.9 %all-to-all-start.4 = ((bf16[32,648,128]{2,1,0:T(8,128)(2,1)}), bf16[32,648,128]{2,1,0:T(8,128)(2,1)}, u32[]{:S(2)}, u32[]{:S(2)}) async-start(bf16[32,648,128]{2,1,0:T(8,128)(2,1)} %pad_maximum_fusion.1), calls=%async_computation.4 | async-start | bytes 10616832 | tf_op jit(solution)/shard_map/all_to_all | solution.py:165
  230.9 3.6 copy-start.20
  241.0 8.8 %slice-start = ((s8[4718592]{0:T(1024)(128)(4,1)}), s8[524288]{0:T(1024)(128)(4,1)S(1)}, s32[]{:S(2)}) async-start(s8[4718592]{0:T(1024)(128)(4,1)} %bitcast.236), calls=%async_computation.7 | async-start | bytes 1048576
  242.4 2.5 copy-start.15
  244.9 4.9 %slice-start.1 = ((s8[4718592]{0:T(1024)(128)(4,1)}), s8[4194304]{0:T(1024)(128)(4,1)S(1)}, s32[]{:S(2)}) async-start(s8[4718592]{0:T(1024)(128)(4,1)} %bitcast.236), calls=%async_computation.8 | async-start | bytes 8388608
  249.9 1.5 copy-start.29
  249.9 1.7 copy-start.3
  251.4 1.3 copy-start.4
  251.4 1.4 copy-start.13
  252.6 2.5 copy-start.25
  253.9 1.3 copy-start.8
  253.9 1.3 copy-start.40
  253.9 1.3 copy-start.42
  253.9 1.3 copy-start.44
  253.9 1.3 copy-start.46
  253.9 1.3 copy-start.48
  253.9 1.3 copy-start.59
  300.8 80.0 %all-to-all-start.3 = ((bf16[32,648,128]{2,1,0:T(8,128)(2,1)}), bf16[32,648,128]{2,1,0:T(8,128)(2,1)}, u32[]{:S(2)}, u32[]{:S(2)}) async-start(bf16[32,648,128]{2,1,0:T(8,128)(2,1)} %pad_maximum_fusion), calls=%async_computation.3 | async-start | bytes 10616832 | tf_op jit(solution)/shard_map/all_to_all | solution.py:165
  312.0 79.5 %all-gather.7.cloned.1.call-start = ((), (), s32[]{:S(2)}) async-start(), calls=%async_computation.6 | async-start | bytes 1658880 | tf_op jit(solution)/shard_map/all_gather | solution.py:167
  316.2 68.7 %copy-start.26 = (bf16[8,72,384]{2,1,0:T(8,128)(2,1)S(1)}, bf16[8,72,384]{2,1,0:T(8,128)(2,1)}, u32[]{:S(2)}) copy-start(bf16[8,72,384]{2,1,0:T(8,128)(2,1)} %copy-done.25) | copy-start | bytes 1327108
  316.2 100.9 %all-gather.5.cloned.1.call-start = ((), (), s32[]{:S(2)}) async-start(), calls=%async_computation.5 | async-start | bytes 1658880 | tf_op jit(solution)/shard_map/all_gather | solution.py:167
  384.9 4.8 %copy-start.9 = (f32[384,1152]{1,0:T(8,128)S(1)}, f32[384,1152]{1,0:T(8,128)}, u32[]{:S(2)}) copy-start(f32[384,1152]{1,0:T(8,128)} %reshape.910) | copy-start | bytes 5308420
  (5 other events, 3.2 us)
Sparse Core Ops, SparseCore 0:
  316.3 66.3 all-gather.6
  385.0 31.9 all-gather.4
